TPU v7x, 32 devices: a whole 2x2x4 slice. The times are simulated.
32 devices in a mesh: fsdp: 8 (over z, core), head: 4 (over y, x).
Axes of the slice: x: 2, y: 2, z: 4, core: 2. Of those that a mesh axis runs over, the one named last changes fastest.
Arguments:
- tokens: bfloat16 [2048, 4096], P('fsdp'), may hold values from -6 to 6
- zx_weight: bfloat16 [4096, 128, 128], P('fsdp', 'head'), may hold values from -0.09375 to 0.09375
- dt_weight: bfloat16 [4096, 128], P('fsdp', 'head'), may hold values from -0.09375 to 0.09375
- bc_weight: bfloat16 [4096, 1024], P('fsdp'), may hold values from -0.09375 to 0.09375
- conv_x: float32 [4, 8192], P(None, 'head'), may hold values from -2 to 2
- conv_bc: float32 [4, 1024], replicated, may hold values from -2 to 2
- a_log: float32 [128], P('head'), may hold values from -5 to 0.5
- dt_bias: float32 [128], P('head'), may hold values from -4 to 0
- d_skip: float32 [128], P('head'), may hold values from 0.5 to 2
- norm_gain: float32 [8192], P('head'), may hold values from 0.1 to 1.9
- out_weight: bfloat16 [8192, 4096], P('head'), may hold values from -0.09375 to 0.09375
Outputs:
- mixed: bfloat16 [2048, 4096], P('fsdp', 'head')
All inputs are finite; a program needn't handle non-finite values.
Results may differ from a plain program's by a relative error of at most 0.015.
Values may be sent and summed in bfloat16 or wider, within the bound.
A program may use at most 128 MiB of HBM per device.

v0:
```python
import jax
import jax.numpy as jnp
from jax import lax
from jax.sharding import PartitionSpec as P

G = 4
LEN = 256


def settle(values):
    return lax.optimization_barrier(values.astype(jnp.bfloat16))


def causal(values, kernel, seq_len):
    columns = values.shape[1]
    seqs = values.reshape(-1, seq_len, columns).astype(jnp.float32)
    taps = kernel.shape[0]
    padded = jnp.pad(seqs, ((0, 0), (taps - 1, 0), (0, 0)))
    total = jnp.zeros(seqs.shape, jnp.float32)
    for tap in range(taps):
        total = total + kernel[tap] * padded[:, tap : tap + seq_len]
    return settle(jax.nn.silu(total).reshape(-1, columns))


def on_device(
    tokens,
    zx_weight,
    dt_weight,
    bc_weight,
    conv_x,
    conv_bc,
    a_log,
    dt_bias,
    d_skip,
    norm_gain,
    out_weight,
):
    tok_rows = tokens.shape[0]
    heads_here = zx_weight.shape[1]
    head_size = zx_weight.shape[2] // 2
    n_head = lax.axis_size("head")
    head_pos = lax.axis_index("head")
    per_group = n_head // G
    group_id = head_pos // per_group
    group_cols = bc_weight.shape[1] // G
    state = group_cols // 2
    piece_cols = group_cols // per_group
    bc_part = lax.dynamic_slice_in_dim(bc_weight, head_pos * piece_cols, piece_cols, 1)
    flat_zx = zx_weight.reshape(zx_weight.shape[0], heads_here * 2 * head_size)
    zx_acc = jnp.dot(
        tokens,
        lax.all_gather(flat_zx, "fsdp", axis=0, tiled=True),
        preferred_element_type=jnp.float32,
    )
    dt_acc = jnp.dot(
        tokens,
        lax.all_gather(dt_weight, "fsdp", axis=0, tiled=True),
        preferred_element_type=jnp.float32,
    )
    bc_acc = jnp.dot(
        tokens,
        lax.all_gather(bc_part, "fsdp", axis=0, tiled=True),
        preferred_element_type=jnp.float32,
    )
    zx = settle(zx_acc).reshape(tok_rows, heads_here, 2, head_size)
    dt_raw = settle(dt_acc)
    bc_raw = settle(bc_acc)
    gathered = lax.all_gather(bc_raw, "head", axis=1, tiled=True)
    bc_raw = lax.dynamic_slice_in_dim(gathered, group_id * group_cols, group_cols, 1)
    channels = heads_here * head_size
    gate = zx[:, :, 0, :].astype(jnp.float32).reshape(tok_rows, channels)
    xin = zx[:, :, 1, :].reshape(tok_rows, channels)
    xconv = causal(xin, conv_x, LEN)
    conv_group = lax.dynamic_slice_in_dim(conv_bc, group_id * group_cols, group_cols, 1)
    bconv = causal(bc_raw, conv_group, LEN)
    count = tok_rows // LEN
    steps = jax.nn.softplus(dt_raw.astype(jnp.float32) + dt_bias).reshape(count, LEN, heads_here)
    cum = jnp.cumsum(-steps * jnp.exp(a_log), axis=1)
    seg = cum[:, :, None, :] - cum[:, None, :, :]
    lower = jnp.arange(LEN)[:, None] >= jnp.arange(LEN)[None, :]
    decay = jnp.exp(jnp.where(lower[None, :, :, None], seg, -1e30))
    bseq = bconv[:, :state].reshape(count, LEN, state)
    cseq = bconv[:, state:].reshape(count, LEN, state)
    inner = jnp.einsum("btn,bsn->bts", cseq, bseq, preferred_element_type=jnp.float32)
    weights = inner[..., None] * decay * steps[:, None, :, :]
    xval = xconv.astype(jnp.float32).reshape(count, LEN, heads_here, head_size)
    ys = jnp.einsum("btsh,bshp->bthp", weights, xval, precision=lax.Precision.HIGHEST)
    ys = ys + d_skip[None, None, :, None] * xval
    gated = ys.reshape(tok_rows, channels) * jax.nn.silu(gate)
    local_sq = jnp.sum(gated * gated, axis=1)
    picks = jnp.arange(G)[None, :] == group_id
    totals = lax.psum(jnp.where(picks, local_sq[:, None], 0.0), "head")
    mine = jnp.sum(jnp.where(picks, totals, 0.0), axis=1)
    meansq = mine / (per_group * channels)
    normed = (gated / jnp.sqrt(meansq + 1e-05)[:, None] * norm_gain).astype(jnp.bfloat16)
    partial_out = jnp.dot(normed, out_weight, preferred_element_type=jnp.float32)
    return lax.psum_scatter(
        partial_out.astype(jnp.bfloat16), "head", scatter_dimension=1, tiled=True
    )


def solution(mesh):
    in_specs = (
        P("fsdp", None),
        P("fsdp", "head", None),
        P("fsdp", "head"),
        P("fsdp", None),
        P(None, "head"),
        P(),
        P("head"),
        P("head"),
        P("head"),
        P("head"),
        P("head", None),
    )
    out_specs = P("fsdp", "head")
    return jax.shard_map(
        on_device, mesh=mesh, in_specs=in_specs, out_specs=out_specs, check_vma=False
    )
```

profile of v0, /device:TPU:10, one launch (start us, length us, event | category | flops | bytes accessed | tf_op | source)
XLA Modules:
  0.0 424.6 jit_solution(4114213936495806850)
XLA Ops:
  6.5 0.0 copy-start
  6.5 0.0 all-gather.5.cloned.1.call-start
  6.5 1.8 constant_dynamic-slice_fusion.1
  8.4 0.0 all-gather.5.cloned.1.call-update
  8.4 0.0 all-gather.3.cloned.1.call-start
  8.4 8.4 %copy.34 = bf16[64,8,32,128]{3,1,2,0:T(8,128)(2,1)} copy(bf16[64,8,32,128]{3,2,1,0:T(8,128)(2,1)} %bitcast.114) | data formatting | bytes 8388608
  16.8 0.0 all-gather.3.cloned.1.call-update
  16.9 0.0 copy-start.5
  16.9 0.0 copy-start.3
  16.9 0.0 reduce-scatter.2.cloned.1.call-start
  16.9 0.6 copy-done.6
  17.5 0.1 copy-done.2
  17.6 15.4 %all_gather.15 = bf16[4096,32]{0,1:T(8,128)(2,1)S(1)} all-gather(bf16[512,32]{0,1:T(8,128)(2,1)S(1)} %copy-done.2), channel_id=1, replica_groups=mesh['fsdp'=8,'head'=4] {'fsdp'}, dimensions={0}, use_global_device_ids=true | all-gather | bytes 294912 | tf_op jit(solution)/shard_map/all_gather | solution.py:57
  33.0 0.0 copy-done
  33.0 0.7 convolution_convert_fusion.3
  33.7 0.0 copy-done.5
  33.7 0.1 multiply_bitcast_fusion
  33.8 0.6 reduce-window.6
  34.5 0.2 slice_reduce_fusion
  34.7 0.1 copy.25
  34.7 0.1 broadcast.123
  34.9 0.9 constant_dynamic-slice_fusion
  35.9 0.0 copy-done.3
  35.9 5.4 %all-gather.5.cloned.1.call-done = bf16[4096,256]{1,0:T(8,128)(2,1)} async-done(((bf16[512,256]{1,0:T(8,128)(2,1)}), bf16[4096,256]{1,0:T(8,128)(2,1)}) %all-gather.5.cloned.1.call-update) | async-done | bytes 2097168 | tf_op jit(solution)/shard_map/all_gather | solution.py:62
  41.3 2.3 fusion.32
  43.7 10.2 %all_gather.14 = bf16[256,1024]{0,1:T(8,128)(2,1)S(1)} all-gather(bf16[256,256]{0,1:T(8,128)(2,1)S(1)} %fusion.32), channel_id=1, replica_groups=mesh['fsdp'=8,'head'=4] {'head'}, dimensions={1}, use_global_device_ids=true | all-gather | bytes 655360 | tf_op jit(solution)/shard_map/all_gather | solution.py:68
  53.9 0.4 fusion.41
  54.3 0.2 fusion.42
  54.5 273.8 %all-gather.3.cloned.1.call-done = bf16[4096,4096]{1,0:T(8,128)(2,1)} async-done(((bf16[512,4096]{1,0:T(8,128)(2,1)}), bf16[4096,4096]{1,0:T(8,128)(2,1)}) %all-gather.3.cloned.1.call-update) | async-done | bytes 33554448 | tf_op jit(solution)/shard_map/all_gather | solution.py:52
  328.3 16.6 %convolution_convert_fusion = bf16[256,4096]{1,0:T(8,128)(2,1)} fusion(bf16[256,4096]{1,0:T(8,128)(2,1)S(1)} %copy-done, bf16[4096,4096]{1,0:T(8,128)(2,1)} %all-gather.3.cloned.1.call-done), kind=kOutput, calls=%fused_computation.6 | convolution fusion | flops 8590983168 | bytes 37748736 | tf_op jit(solution)/shard_map/dot_general | solution.py:50
  345.0 3.3 copy.22
  348.2 0.1 slice.82
  348.3 0.2 convert.4
  348.5 0.0 copy-start.7
  348.5 3.2 fusion.33
  351.7 0.0 copy-done.7
  351.7 0.0 copy-start.4
  351.7 7.9 %fusion.29 = (f32[256]{0:T(256)S(1)}, f32[1,256,32,64]{1,3,2,0:T(8,128)}) fusion(bf16[256,32,2,64]{0,3,2,1:T(8,128)(2,1)S(1)} %bitcast.111, bf16[1,256,32,64]{1,3,2,0:T(8,128)(2,1)S(1)} %bitcast.115, f32[32]{0:T(128)S(1)} %copy-done.7, bf16[256,32,64]{0,2,1:T(8,128)(2,1)S(1)} %bitcast.116, f32[256,32]{0,1:T(8,128)S(1)} %get-tuple-element.10, ...), kind=kOutput, calls=%fused_computation.42 | convolution fusion | flops 1624768256 | bytes 5670400 | tf_op jit(solution)/shard_map/btsh,bshp->bthp/dot_general | solution.py:87
  359.6 0.1 broadcast_select_fusion
  359.7 8.0 %psum.7 = f32[256,4]{0,1:T(4,128)S(1)} all-reduce(f32[256,4]{0,1:T(4,128)S(1)} %broadcast_select_fusion), channel_id=1, replica_groups=mesh['fsdp'=8,'head'=4] {'head'}, use_global_device_ids=true, to_apply=%region_3.4 | all-reduce | flops 1024 | bytes 8192 | tf_op jit(solution)/shard_map/psum | solution.py:92
  367.7 0.1 select_reduce_fusion
  367.8 0.0 copy-done.4
  367.8 2.3 multiply_convert_fusion
  370.1 0.0 copy-start.1
  370.1 11.7 %convolution_convert_fusion.1 = bf16[256,4096]{1,0:T(8,128)(2,1)} fusion(bf16[256,2048]{0,1:T(8,128)(2,1)S(1)} %multiply_convert_fusion, bf16[2048,4096]{1,0:T(8,128)(2,1)} %param.21), kind=kOutput, calls=%fused_computation.7 | convolution fusion | flops 4296015872 | bytes 19922944 | tf_op jit(solution)/shard_map/dot_general | solution.py:96
  381.8 0.0 reduce-scatter.2.cloned.1.call-update
  381.8 36.3 %reduce-scatter.2.cloned.1.call-done = bf16[256,1024]{1,0:T(8,128)(2,1)} async-done(((bf16[256,4096]{1,0:T(8,128)(2,1)}), bf16[256,1024]{1,0:T(8,128)(2,1)}) %reduce-scatter.2.cloned.1.call-update) | async-done | bytes 524304 | tf_op jit(solution)/shard_map/reduce_scatter | solution.py:97
  418.1 0.0 copy-done.1
  (14 shorter events, 0.2 us)
Async XLA Ops:
  6.5 26.4 %copy-start = (bf16[256,4096]{1,0:T(8,128)(2,1)S(1)}, bf16[256,4096]{1,0:T(8,128)(2,1)}, u32[]{:S(2)}) copy-start(bf16[256,4096]{1,0:T(8,128)(2,1)} %param.11) | copy-start | bytes 6291460
  6.5 34.8 %all-gather.5.cloned.1.call-start = ((), (), s32[]{:S(2)}) async-start(), calls=%async_computation.2 | async-start | bytes 2359296 | tf_op jit(solution)/shard_map/all_gather | solution.py:62
  8.4 320.0 %all-gather.3.cloned.1.call-start = ((), (), s32[]{:S(2)}) async-start(), calls=%async_computation.1 | async-start | bytes 37748736 | tf_op jit(solution)/shard_map/all_gather | solution.py:52
  16.8 0.7 copy-start.6
  16.8 0.8 copy-start.2
  16.9 16.9 %copy-start.5 = (f32[32]{0:T(128)S(1)}, f32[32]{0:T(128)}, u32[]{:S(2)}) copy-start(f32[32]{0:T(128)} %param.18) | copy-start | bytes 388
  16.9 19.0 %copy-start.3 = (f32[4,2048]{1,0:T(4,128)S(1)}, f32[4,2048]{1,0:T(4,128)}, u32[]{:S(2)}) copy-start(f32[4,2048]{1,0:T(4,128)} %param.15) | copy-start | bytes 98308
  16.9 401.2 %reduce-scatter.2.cloned.1.call-start = ((), (), s32[]{:S(2)}) async-start(), calls=%async_computation.3 | async-start | bytes 2621440 | tf_op jit(solution)/shard_map/reduce_scatter | solution.py:97
  348.5 3.2 copy-start.7
  351.7 16.1 %copy-start.4 = (f32[2048]{0:T(1024)S(1)}, f32[2048]{0:T(1024)}, u32[]{:S(2)}) copy-start(f32[2048]{0:T(1024)} %param.20) | copy-start | bytes 24580
  370.1 48.0 %copy-start.1 = (bf16[256,4096]{1,0:T(8,128)(2,1)S(1)}, bf16[256,4096]{1,0:T(8,128)(2,1)}, u32[]{:S(2)}) copy-start(bf16[256,4096]{1,0:T(8,128)(2,1)} %param.11) | copy-start | bytes 6291460
Sparse Core Ops, SparseCore 0:
  9.0 32.3 all-gather.4
  42.9 285.3 all-gather.2
  382.0 36.0 reduce-scatter.1
where the time goes:
time: 427 us; the launch traced here: 425 us
  waiting for transfers between devices  316 us (74%)
  matrix products  39.5 us (9%)
  blocking collectives  33.6 us (8%)
  local copies, waits for them, and re-layouts  15.6 us (4%)
  between operations  13.3 us (3%)
  other arithmetic  7.08 us (2%)
    all_gather x1, waiting for transfers between devices, on_device(): lax.all_gather(flat_zx, 'fsdp', axis=0, tiled=True)  274 us
    reduce_scatter x1, waiting for transfers between devices, on_device(): lax.psum_scatter(partial_out.astype(jnp.bfloat16), 'head', scatter_dimens...  36.3 us
    dot_general x1, matrix products, on_device(): jnp.dot(tokens, lax.all_gather(flat_zx, 'fsdp', axis=0, tiled=True), pref...  16.6 us
    all_gather x1, blocking collectives, on_device(): lax.all_gather(dt_weight, 'fsdp', axis=0, tiled=True)  15.4 us
    dot_general x1, matrix products, on_device(): jnp.dot(normed, out_weight, preferred_element_type=jnp.float32)  11.7 us
    all_gather x1, blocking collectives, on_device(): gathered = lax.all_gather(bc_raw, 'head', axis=1, tiled=True)  10.2 us
    unnamed x18, local copies, waits for them, and re-layouts  9.12 us
  transfers between devices with their start and end apart: 3, of which 3 were waited for; matrix products, arithmetic and copies ran while one was open for 3% of the time, Pallas kernels for 0%

commit v1 on v0

v1 whole, which is shorter than its diff:
```python
import functools
import math

import jax
import jax.numpy as jnp
from jax import lax
from jax.experimental import pallas as pl
from jax.experimental.pallas import tpu as pltpu
from jax.sharding import PartitionSpec as P

G = 4
LEN = 256
MESH = pl.DeviceIdType.MESH


def settle(values):
    return lax.optimization_barrier(values.astype(jnp.bfloat16))


def remote(src, dst, send, recv, f, h):
    return pltpu.make_async_remote_copy(
        src_ref=src, dst_ref=dst, send_sem=send, recv_sem=recv, device_id=(f, h), device_id_type=MESH
    )


def project_kernel(
    chips, share, chunks, width, tok_ref, w_ref, out_ref, x, wv, buf, stage,
    local_sem, w_sem, own_sem, z_sem, h_sem, s_sem, line_send, line_recv, fin_sem,
):
    f = lax.axis_index("fsdp")
    h = lax.axis_index("head")
    z, c = lax.div(f, 2), lax.rem(f, 2)
    sib = z * 2 + 1 - c
    part = lax.rem(h, share)
    base = h - part
    tok = tok_ref.shape[0]
    depth = w_ref.shape[1]
    cols = w_ref.shape[2]
    rows = 2 * tok // chunks
    piece = tok // share

    barrier = pltpu.get_barrier_semaphore()
    for o in range(1, chips):
        pl.semaphore_signal(barrier, inc=1, device_id=(lax.rem(z + o, chips) * 2 + c, h), device_id_type=MESH)
    pl.semaphore_signal(barrier, inc=1, device_id=(sib, h), device_id_type=MESH)
    for k in range(1, share):
        pl.semaphore_signal(barrier, inc=1, device_id=(f, base + lax.rem(part + k, share)), device_id_type=MESH)
    pl.semaphore_wait(barrier, chips - 1 + 1 + share - 1)

    def spot(chip, core, p):
        return x.at[pl.ds(pl.multiple_of((chip * 2 + core) * tok + p * piece, 16), piece), :]

    def z_copy(o):
        to = lax.rem(z + o, chips)
        src = tok_ref.at[
            pl.ds(pl.multiple_of(part * piece, 16), piece), pl.ds(pl.multiple_of(to * 2 * depth, 128), 2 * depth)
        ]
        return remote(src, spot(z, c, part), z_sem.at[0, o], z_sem.at[1, o], to * 2 + c, h)

    def h_copy(o, k):
        at = spot(lax.rem(z - o + chips, chips), c, part)
        return remote(at, at, h_sem.at[0, o, k], h_sem.at[1, o, k], f, base + lax.rem(part + k, share))

    def s_copy(o, k):
        at = spot(lax.rem(z - o + chips, chips), c, lax.rem(part - k + share, share))
        return remote(at, at, s_sem.at[0, o, k], s_sem.at[1, o, k], sib, h)

    @pl.loop(1, chips)
    def _(o):
        z_copy(o).start()

    mine = tok_ref.at[:, pl.ds(pl.multiple_of(z * 2 * depth, 128), 2 * depth)]
    my_rows = x.at[pl.ds(pl.multiple_of(f * tok, 16), tok), :]
    own = pltpu.make_async_copy(mine, my_rows, local_sem.at[0])
    own.start()
    own_out = remote(mine, my_rows, own_sem.at[0], own_sem.at[1], sib, h)
    own_out.start()
    w_rows = wv.at[pl.ds(pl.multiple_of(c * depth, 16), depth), :]
    w_own = pltpu.make_async_copy(w_ref.at[c], w_rows, local_sem.at[1])
    w_own.start()
    w_out = remote(w_ref.at[1 - c], w_rows, w_sem.at[0], w_sem.at[1], sib, h)
    w_out.start()

    @pl.loop(1, chips)
    def _(o):
        z_copy(o).wait_recv()
        for k in range(1, share):
            h_copy(o, k).start()
        s_copy(o, 0).start()

    @pl.loop(1, chips)
    def _(o):
        for k in range(1, share):
            h_copy(o, k).wait_recv()
            s_copy(o, k).start()

    own.wait()
    w_own.wait()
    own_out.wait()
    w_out.wait()

    @pl.loop(1, chips)
    def _(o):
        z_copy(o).wait_send()
        for k in range(1, share):
            h_copy(o, k).wait_send()
        for k in range(share):
            s_copy(o, k).wait()

    def partial(d, ch, j):
        left = x[pl.ds(pl.multiple_of(d * 2 * tok + ch * rows, 16), rows), :]
        right = wv[:, pl.ds(pl.multiple_of(j * width, 128), width)]
        return jnp.dot(left, right, preferred_element_type=jnp.float32)

    total = (chips - 1) * chunks

    def line(way, d, ch, i):
        to = z + 1 - 2 * way
        at = buf.at[way, d, pl.ds(pl.multiple_of(ch * rows, 16), rows), :]
        return remote(at, at, line_send.at[way, i], line_recv.at[way, i], to * 2 + c, h)

    def where(way, i):
        d = lax.div(i, chunks)
        return (chips - 1 - d if way == 0 else d), lax.rem(i, chunks)

    @pl.loop(0, total)
    def _(i):
        for way in (0, 1):
            d, ch = where(way, i)
            active = z < d if way == 0 else z > d
            first = z == 0 if way == 0 else z == chips - 1

            @pl.when(active)
            def _(way=way, d=d, ch=ch, first=first):
                at = pl.ds(pl.multiple_of(ch * rows, 16), rows)

                @pl.when(jnp.logical_not(first))
                def _():
                    line(way, d, ch, i).wait_recv()

                    @pl.loop(0, cols // width)
                    def _(j):
                        to = pl.ds(pl.multiple_of(j * width, 128), width)
                        got = buf[way, d, at, to].astype(jnp.float32)
                        buf[way, d, at, to] = (got + partial(d, ch, j)).astype(jnp.bfloat16)

                @pl.when(first)
                def _():
                    @pl.loop(0, cols // width)
                    def _(j):
                        to = pl.ds(pl.multiple_of(j * width, 128), width)
                        buf[way, d, at, to] = partial(d, ch, j).astype(jnp.bfloat16)

                @pl.when(i >= 2)
                def _():
                    d2, ch2 = where(way, i - 2)
                    line(way, d2, ch2, i - 2).wait_send()

                line(way, d, ch, i).start()

    half = chunks // 2

    def finish(ch):
        at = stage.at[pl.ds(pl.multiple_of(lax.rem(ch, half) * rows, 16), rows), :]
        to = out_ref.at[c, pl.ds(pl.multiple_of(lax.rem(ch, half) * rows, 16), rows), :]
        return remote(at, to, fin_sem.at[0, lax.rem(ch, half)], fin_sem.at[1, lax.rem(ch, half)], sib, h)

    @pl.loop(0, chunks)
    def _(ch):
        at = pl.ds(pl.multiple_of(ch * rows, 16), rows)

        @pl.when(z > 0)
        def _():
            line(0, z, ch, (chips - 1 - z) * chunks + ch).wait_recv()

        @pl.when(z < chips - 1)
        def _():
            line(1, z, ch, z * chunks + ch).wait_recv()

        here = lax.div(ch, half) == c
        to_rows = pl.ds(pl.multiple_of(lax.rem(ch, half) * rows, 16), rows)

        @pl.loop(0, cols // width)
        def _(j):
            to = pl.ds(pl.multiple_of(j * width, 128), width)
            stage2 = partial(z, ch, j)

            def both(v):
                @pl.when(here)
                def _():
                    out_ref[c, to_rows, to] = v.astype(jnp.bfloat16)

                @pl.when(jnp.logical_not(here))
                def _():
                    stage[to_rows, to] = v.astype(jnp.bfloat16)

            @pl.when(z == 0)
            def _():
                both(stage2 + buf[1, z, at, to].astype(jnp.float32))

            @pl.when(z == chips - 1)
            def _():
                both(stage2 + buf[0, z, at, to].astype(jnp.float32))

            @pl.when(jnp.logical_and(z > 0, z < chips - 1))
            def _():
                both(stage2 + buf[0, z, at, to].astype(jnp.float32) + buf[1, z, at, to].astype(jnp.float32))

        @pl.when(jnp.logical_not(here))
        def _():
            finish(ch).start()

    @pl.loop(0, half)
    def _(ch):
        finish(ch).wait()

    for way in (0, 1):
        count = (chips - 1 - z if way == 0 else z) * chunks

        @pl.when(count > 0)
        def _(way=way, count=count):
            for back in (2, 1):
                d2, ch2 = where(way, count - back)
                line(way, d2, ch2, count - back).wait_send()


def project(tokens, weights, n_fsdp, n_head):
    chips = n_fsdp // 2
    share = math.gcd(n_head, 4)
    tok = tokens.shape[0]
    depth, cols = weights.shape[1:]
    chunks = 4
    width = max(w for w in range(128, 769, 128) if cols % w == 0)
    total = (chips - 1) * chunks
    return pl.pallas_call(
        functools.partial(project_kernel, chips, share, chunks, width),
        out_shape=jax.ShapeDtypeStruct((2, tok, cols), jnp.bfloat16),
        in_specs=[pl.BlockSpec(memory_space=pl.ANY)] * 2,
        out_specs=pl.BlockSpec(memory_space=pltpu.VMEM),
        scratch_shapes=[
            pltpu.VMEM((chips * 2 * tok, 2 * depth), jnp.bfloat16),
            pltpu.VMEM((2 * depth, cols), jnp.bfloat16),
            pltpu.VMEM((2, chips, 2 * tok, cols), jnp.bfloat16),
            pltpu.VMEM((tok, cols), jnp.bfloat16),
            pltpu.SemaphoreType.DMA((2,)),
            pltpu.SemaphoreType.DMA((2,)),
            pltpu.SemaphoreType.DMA((2,)),
            pltpu.SemaphoreType.DMA((2, chips)),
            pltpu.SemaphoreType.DMA((2, chips, share)),
            pltpu.SemaphoreType.DMA((2, chips, share)),
            pltpu.SemaphoreType.DMA((2, total)),
            pltpu.SemaphoreType.DMA((2, total)),
            pltpu.SemaphoreType.DMA((2, chunks // 2)),
        ],
        compiler_params=pltpu.CompilerParams(
            collective_id=0, has_side_effects=True, vmem_limit_bytes=48 * 1024 * 1024
        ),
    )(tokens, weights)


def causal(values, kernel, seq_len):
    columns = values.shape[1]
    seqs = values.reshape(-1, seq_len, columns).astype(jnp.float32)
    taps = kernel.shape[0]
    padded = jnp.pad(seqs, ((0, 0), (taps - 1, 0), (0, 0)))
    total = jnp.zeros(seqs.shape, jnp.float32)
    for tap in range(taps):
        total = total + kernel[tap] * padded[:, tap : tap + seq_len]
    return settle(jax.nn.silu(total).reshape(-1, columns))


def on_device(
    tokens,
    zx_weight,
    dt_weight,
    bc_weight,
    conv_x,
    conv_bc,
    a_log,
    dt_bias,
    d_skip,
    norm_gain,
    out_weight,
):
    tok_rows = tokens.shape[0]
    heads_here = zx_weight.shape[1]
    head_size = zx_weight.shape[2] // 2
    n_head = lax.axis_size("head")
    n_fsdp = lax.axis_size("fsdp")
    head_pos = lax.axis_index("head")
    per_group = n_head // G
    group_id = head_pos // per_group
    group_cols = bc_weight.shape[1] // G
    state = group_cols // 2
    piece_cols = group_cols // per_group
    depth = zx_weight.shape[0]
    bc_part = lax.dynamic_slice_in_dim(bc_weight, head_pos * piece_cols, piece_cols, 1)
    flat_zx = zx_weight.reshape(depth, heads_here * 2 * head_size)
    zx_half, bc_half, dt_half = heads_here * head_size, piece_cols // 2, heads_here // 2
    used = zx_half + bc_half + dt_half
    cols = -(-used // 128) * 128
    blank = jnp.zeros((depth, cols - used), jnp.bfloat16)
    weights = jnp.stack(
        [
            jnp.concatenate(
                [
                    flat_zx[:, c * zx_half : (c + 1) * zx_half],
                    bc_part[:, c * bc_half : (c + 1) * bc_half],
                    dt_weight[:, c * dt_half : (c + 1) * dt_half],
                    blank,
                ],
                axis=1,
            )
            for c in (0, 1)
        ]
    )
    got = project(tokens, weights, n_fsdp, n_head)
    zx = jnp.concatenate([got[0, :, :zx_half], got[1, :, :zx_half]], axis=1).reshape(
        tok_rows, heads_here, 2, head_size
    )
    bc_raw = jnp.concatenate([got[0, :, zx_half : zx_half + bc_half], got[1, :, zx_half : zx_half + bc_half]], axis=1)
    dt_raw = jnp.concatenate([got[0, :, zx_half + bc_half : used], got[1, :, zx_half + bc_half : used]], axis=1)
    if per_group > 1:
        gathered = lax.all_gather(bc_raw, "head", axis=1, tiled=True)
        bc_raw = lax.dynamic_slice_in_dim(gathered, group_id * group_cols, group_cols, 1)
    channels = heads_here * head_size
    gate = zx[:, :, 0, :].astype(jnp.float32).reshape(tok_rows, channels)
    xin = zx[:, :, 1, :].reshape(tok_rows, channels)
    xconv = causal(xin, conv_x, LEN)
    conv_group = lax.dynamic_slice_in_dim(conv_bc, group_id * group_cols, group_cols, 1)
    bconv = causal(bc_raw, conv_group, LEN)
    count = tok_rows // LEN
    steps = jax.nn.softplus(dt_raw.astype(jnp.float32) + dt_bias).reshape(count, LEN, heads_here)
    lower = jnp.arange(LEN)[:, None] >= jnp.arange(LEN)[None, :]
    cum = jnp.einsum(
        "ts,bsh->bth", lower.astype(jnp.float32), -steps * jnp.exp(a_log), precision=lax.Precision.HIGHEST
    )
    seg = cum[:, :, None, :] - cum[:, None, :, :]
    decay = jnp.exp(jnp.where(lower[None, :, :, None], seg, -1e30))
    bseq = bconv[:, :state].reshape(count, LEN, state)
    cseq = bconv[:, state:].reshape(count, LEN, state)
    inner = jnp.einsum("btn,bsn->bts", cseq, bseq, preferred_element_type=jnp.float32)
    weights = inner[..., None] * decay * steps[:, None, :, :]
    xval = xconv.astype(jnp.float32).reshape(count, LEN, heads_here, head_size)
    ys = jnp.einsum("btsh,bshp->bthp", weights, xval, precision=lax.Precision.HIGHEST)
    ys = ys + d_skip[None, None, :, None] * xval
    gated = ys.reshape(tok_rows, channels) * jax.nn.silu(gate)
    local_sq = jnp.sum(gated * gated, axis=1)
    if per_group > 1:
        picks = jnp.arange(G)[None, :] == group_id
        totals = lax.psum(jnp.where(picks, local_sq[:, None], 0.0), "head")
        local_sq = jnp.sum(jnp.where(picks, totals, 0.0), axis=1)
    meansq = local_sq / (per_group * channels)
    normed = (gated / jnp.sqrt(meansq + 1e-05)[:, None] * norm_gain).astype(jnp.bfloat16)
    partial_out = jnp.dot(normed, out_weight, preferred_element_type=jnp.float32)
    return lax.psum_scatter(
        partial_out.astype(jnp.bfloat16), "head", scatter_dimension=1, tiled=True
    )


def solution(mesh):
    in_specs = (
        P("fsdp", None),
        P("fsdp", "head", None),
        P("fsdp", "head"),
        P("fsdp", None),
        P(None, "head"),
        P(),
        P("head"),
        P("head"),
        P("head"),
        P("head"),
        P("head", None),
    )
    out_specs = P("fsdp", "head")
    return jax.shard_map(
        on_device, mesh=mesh, in_specs=in_specs, out_specs=out_specs, check_vma=False
    )
```

time: 427 us -> 310 us (0.73)
  waiting for transfers between devices: 316 us -> 33.5 us
  Pallas kernels: 0 us -> 210 us
  blocking collectives: 33.6 us -> 0 us
  matrix products: 39.5 us -> 19.4 us
  local copies, waits for them, and re-layouts: 15.6 us -> 21.2 us
    all_gather x2 -> x0, waiting for transfers between devices: 279 us -> none  [the longest x1 274 us: on_device(): lax.all_gather(flat_zx, 'fsdp', axis=0, tiled=True)]
    pallas_call x0 -> x1, Pallas kernels: none -> 210 us  [project(): pl.pallas_call(functools.partial(project_kernel, chips, share, chunks, wi...]
    all_gather x2 -> x0, blocking collectives: 25.5 us -> none  [the longest x1 15.4 us: on_device(): lax.all_gather(dt_weight, 'fsdp', axis=0, tiled=True)]
    dot_general x3 -> x1, matrix products: 19.7 us -> 0.28 us  [on_device(): jnp.einsum('ts,bsh->bth', lower.astype(jnp.float32), -steps * jnp.exp(a_l...]
    concatenate x0 -> x5, local copies, waits for them, and re-layouts: none -> 8.43 us  [the longest x2 8.27 us: on_device(): jnp.concatenate([flat_zx[:, c * zx_half:(c + 1) * zx_half], bc_part[:, c...]
    psum x1 -> x0, blocking collectives: 8.01 us -> none  [on_device(): totals = lax.psum(jnp.where(picks, local_sq[:, None], 0.0), 'head')]
    slice x2 -> x9, local copies, waits for them, and re-layouts: 0.23 us -> 4.84 us  [the longest x1 2.27 us: on_device(): flat_zx[:, c * zx_half:(c + 1) * zx_half]]
    unnamed x18 -> x13, local copies, waits for them, and re-layouts: 9.12 us -> 6.96 us
  transfers between devices with their start and end apart: 3 -> 1, of which waited for: 3 -> 1; matrix products, arithmetic and copies ran while one was open for 3% -> 0% of each run, Pallas kernels for 0% -> 0%
where the time goes in v1:
time: 310 us; the launch traced here: 308 us
  Pallas kernels  210 us (68%)
  waiting for transfers between devices  33.5 us (11%)
  local copies, waits for them, and re-layouts  21.2 us (7%)
  matrix products  19.4 us (6%)
  between operations  13.6 us (4%)
  other arithmetic  10.2 us (3%)
    pallas_call x1, Pallas kernels, project(): pl.pallas_call(functools.partial(project_kernel, chips, share, chunks, wi...  210 us
    reduce_scatter x1, waiting for transfers between devices, on_device(): lax.psum_scatter(partial_out.astype(jnp.bfloat16), 'head', scatter_dimens...  33.5 us
    dot_general x1, matrix products, on_device(): jnp.dot(normed, out_weight, preferred_element_type=jnp.float32)  11.6 us
    concatenate x2, local copies, waits for them, and re-layouts, on_device(): jnp.concatenate([flat_zx[:, c * zx_half:(c + 1) * zx_half], bc_part[:, c...  8.27 us
    dot_general x1, matrix products, on_device(): jnp.einsum('btsh,bshp->bthp', weights, xval, precision=lax.Precision.HIGH...  7.33 us
    unnamed x13, local copies, waits for them, and re-layouts  6.96 us
  transfers between devices with their start and end apart: 1, of which 1 were waited for; matrix products, arithmetic and copies ran while one was open for 0% of the time, Pallas kernels for 0%

profile of v1, /device:TPU:10, one launch (start us, length us, event | category | flops | bytes accessed | tf_op | source)
XLA Modules:
  0.0 308.3 jit_solution(5660575179319572013)
XLA Ops:
  6.5 0.0 reduce-scatter.2.cloned.1.call-start
  6.5 6.4 %copy.37 = bf16[64,8,32,128]{3,1,2,0:T(8,128)(2,1)S(1)} copy(bf16[64,8,32,128]{3,2,1,0:T(8,128)(2,1)} %bitcast.98) | data formatting | bytes 8388608
  12.9 0.0 copy-start.1
  12.9 2.3 fusion.44
  15.2 0.0 copy-done.1
  15.2 0.1 copy.24
  15.3 0.1 copy.25
  15.4 1.0 constant_dynamic-slice_fusion.1
  16.5 3.7 %concatenate.41 = bf16[512,2304]{1,0:T(8,128)(2,1)S(1)} concatenate(bf16[512,2048]{1,0:T(8,128)(2,1)} %get-tuple-element.5, bf16[512,128]{1,0:T(8,128)(2,1)S(1)} %get-tuple-element.13, bf16[512,16]{1,0:T(8,128)(2,1)S(1)} %copy.24, bf16[512,112]{1,0:T(8,128)(2,1)S(1)} %broadcast_in_dim.10), dimensions={1} | concatenate | bytes 4718592 | tf_op jit(solution)/shard_map/concatenate | solution.py:305
  20.1 4.6 %concatenate.42 = bf16[512,2304]{1,0:T(8,128)(2,1)} concatenate(bf16[512,2048]{1,0:T(8,128)(2,1)} %get-tuple-element.6, bf16[512,128]{1,0:T(8,128)(2,1)S(1)} %get-tuple-element.14, bf16[512,16]{1,0:T(8,128)(2,1)S(1)} %copy.25, bf16[512,112]{1,0:T(8,128)(2,1)S(1)} %broadcast_in_dim.10), dimensions={1} | concatenate | bytes 4718592 | tf_op jit(solution)/shard_map/concatenate | solution.py:305
  24.7 0.0 copy-start
  24.7 4.4 %pad_maximum_fusion.w_ref = bf16[2,512,2304]{2,1,0:T(8,128)(2,1)} fusion(bf16[1,512,2304]{2,1,0:T(8,128)(2,1)} %bitcast.96, bf16[1,512,2304]{2,1,0:T(8,128)(2,1)S(1)} %bitcast.95), kind=kLoop, calls=%fused_computation.7 | loop fusion | flops 2359296 | bytes 9437184 | tf_op jit(solution)/shard_map/stack | solution.py:303
  29.1 0.0 copy-done
  29.1 210.5 %shard_map.109 = bf16[2,256,2304]{2,1,0:T(8,128)(2,1)S(1)} custom-call(bf16[256,4096]{1,0:T(8,128)(2,1)S(1)} %copy-done, bf16[2,512,2304]{2,1,0:T(8,128)(2,1)} %pad_maximum_fusion.w_ref), custom_call_target="tpu_custom_call" | custom-call | tf_op jit(solution)/shard_map/pallas_call | solution.py:235
  239.6 0.3 fusion.46
  239.9 0.7 iota_compare_fusion
  240.6 0.9 constant_dynamic-slice_fusion
  241.5 0.2 fusion.36
  241.7 0.2 fusion.37
  241.9 0.5 copy.26
  242.4 0.5 copy.27
  242.9 0.1 fusion.32
  243.0 0.0 copy-start.2
  243.1 0.2 convert.4
  243.2 0.6 copy-done.2
  243.8 0.0 copy-start.5
  243.8 0.0 copy-start.4
  243.8 3.2 %fusion.34 = bf16[256,2048]{0,1:T(8,128)(2,1)S(1)} fusion(f32[1,256,2048]{1,2,0:T(8,128)S(1)} %convert.4, f32[2048]{0:T(1024)S(1)} %bitcast.103, f32[2048]{0:T(1024)S(1)} %bitcast.104, f32[2048]{0:T(1024)S(1)} %bitcast.102, f32[2048]{0:T(1024)S(1)} %bitcast.101), kind=kLoop, calls=%fused_computation.49 | loop fusion | flops 6291456 | bytes 3178496 | tf_op jit(solution)/shard_map/convert_element_type | solution.py:17
  247.0 0.1 copy.30
  247.1 0.1 copy.31
  247.2 0.0 copy-done.5
  247.2 0.0 copy-done.4
  247.2 0.1 compare_select_fusion
  247.3 0.3 convolution_bitcast_fusion
  247.6 0.0 copy-start.3
  247.6 7.3 %fusion.29 = (f32[256]{0:T(256)S(1)}, f32[1,256,32,64]{1,3,2,0:T(8,128)S(1)}) fusion(bf16[256,16,2,64]{0,3,2,1:T(8,128)(2,1)S(1)} %bitcast.93, bf16[256,16,2,64]{0,3,2,1:T(8,128)(2,1)S(1)} %bitcast.90, bf16[1,256,32,64]{1,3,2,0:T(8,128)(2,1)S(1)} %bitcast.99, f32[32]{0:T(128)} %param.19, bf16[256,32,64]{0,2,1:T(8,128)(2,1)S(1)} %bitcast.100, ...), kind=kOutput, calls=%fused_computation.44 | convolution fusion | flops 1625292544 | bytes 6685824 | tf_op jit(solution)/shard_map/btsh,bshp->bthp/dot_general | solution.py:345
  255.0 0.0 copy-done.3
  255.0 1.4 multiply_convert_fusion
  256.4 11.6 %convolution_convert_fusion = bf16[256,4096]{1,0:T(8,128)(2,1)} fusion(bf16[256,2048]{0,1:T(8,128)(2,1)S(1)} %multiply_convert_fusion, bf16[2048,4096]{1,0:T(8,128)(2,1)} %param.21), kind=kOutput, calls=%fused_computation.6 | convolution fusion | flops 4296015872 | bytes 19922944 | tf_op jit(solution)/shard_map/dot_general | solution.py:355
  267.9 0.0 reduce-scatter.2.cloned.1.call-update
  268.0 33.5 %reduce-scatter.2.cloned.1.call-done = bf16[256,1024]{1,0:T(8,128)(2,1)} async-done(((bf16[256,4096]{1,0:T(8,128)(2,1)}), bf16[256,1024]{1,0:T(8,128)(2,1)}) %reduce-scatter.2.cloned.1.call-update) | async-done | bytes 524304 | tf_op jit(solution)/shard_map/reduce_scatter | solution.py:356
  (8 shorter events, 0.1 us)
Async XLA Ops:
  6.5 294.9 %reduce-scatter.2.cloned.1.call-start = ((), (), s32[]{:S(2)}) async-start(), calls=%async_computation.1 | async-start | bytes 2621440 | tf_op jit(solution)/shard_map/reduce_scatter | solution.py:356
  12.9 2.3 copy-start.1
  24.7 4.4 %copy-start = (bf16[256,4096]{1,0:T(8,128)(2,1)S(1)}, bf16[256,4096]{1,0:T(8,128)(2,1)}, u32[]{:S(2)}) copy-start(bf16[256,4096]{1,0:T(8,128)(2,1)} %tok_ref.1) | copy-start | bytes 6291460
  243.0 0.8 copy-start.2
  243.8 3.4 %copy-start.5 = (f32[32]{0:T(128)S(1)}, f32[32]{0:T(128)}, u32[]{:S(2)}) copy-start(f32[32]{0:T(128)} %param.17) | copy-start | bytes 388
  243.8 3.4 %copy-start.4 = (f32[32]{0:T(128)S(1)}, f32[32]{0:T(128)}, u32[]{:S(2)}) copy-start(f32[32]{0:T(128)} %param.18) | copy-start | bytes 388
  247.6 7.4 %copy-start.3 = (f32[2048]{0:T(1024)S(1)}, f32[2048]{0:T(1024)}, u32[]{:S(2)}) copy-start(f32[2048]{0:T(1024)} %param.20) | copy-start | bytes 24580
Sparse Core Ops, SparseCore 0:
  268.1 33.3 reduce-scatter.1

commit v2 on v1

--- a/solution.py
+++ b/solution.py
@@ -24,7 +24,7 @@
 
 
 def project_kernel(
-    chips, share, chunks, width, tok_ref, w_ref, out_ref, x, wv, buf, stage,
+    chips, share, chunks, width, tok_ref, w_ref, e_ref, out_ref, x, wv, buf, stage,
     local_sem, w_sem, own_sem, z_sem, h_sem, s_sem, line_send, line_recv, fin_sem,
 ):
     f = lax.axis_index("fsdp")
@@ -34,8 +34,9 @@
     part = lax.rem(h, share)
     base = h - part
     tok = tok_ref.shape[0]
-    depth = w_ref.shape[1]
-    cols = w_ref.shape[2]
+    depth = w_ref.shape[0]
+    main = w_ref.shape[1] // 2
+    cols = main + e_ref.shape[2]
     rows = 2 * tok // chunks
     piece = tok // share
 
@@ -75,11 +76,20 @@
     own.start()
     own_out = remote(mine, my_rows, own_sem.at[0], own_sem.at[1], sib, h)
     own_out.start()
-    w_rows = wv.at[pl.ds(pl.multiple_of(c * depth, 16), depth), :]
-    w_own = pltpu.make_async_copy(w_ref.at[c], w_rows, local_sem.at[1])
+    w_rows = pl.ds(pl.multiple_of(c * depth, 16), depth)
+    w_main, w_ext = wv.at[w_rows, pl.ds(0, main)], wv.at[w_rows, pl.ds(main, cols - main)]
+
+    def half_of(core):
+        return w_ref.at[:, pl.ds(pl.multiple_of(core * main, 128), main)]
+
+    w_own = pltpu.make_async_copy(half_of(c), w_main, local_sem.at[1])
     w_own.start()
-    w_out = remote(w_ref.at[1 - c], w_rows, w_sem.at[0], w_sem.at[1], sib, h)
+    e_own = pltpu.make_async_copy(e_ref.at[c], w_ext, local_sem.at[2])
+    e_own.start()
+    w_out = remote(half_of(1 - c), w_main, w_sem.at[0], w_sem.at[1], sib, h)
     w_out.start()
+    e_out = remote(e_ref.at[1 - c], w_ext, w_sem.at[2], w_sem.at[3], sib, h)
+    e_out.start()
 
     @pl.loop(1, chips)
     def _(o):
@@ -96,8 +106,10 @@
 
     own.wait()
     w_own.wait()
+    e_own.wait()
     own_out.wait()
     w_out.wait()
+    e_out.wait()
 
     @pl.loop(1, chips)
     def _(o):
@@ -224,26 +236,27 @@
                 line(way, d2, ch2, count - back).wait_send()
 
 
-def project(tokens, weights, n_fsdp, n_head):
+def project(tokens, weights, extra, n_fsdp, n_head):
     chips = n_fsdp // 2
     share = math.gcd(n_head, 4)
     tok = tokens.shape[0]
-    depth, cols = weights.shape[1:]
+    depth = weights.shape[0]
+    cols = weights.shape[1] // 2 + extra.shape[2]
     chunks = 4
     width = max(w for w in range(128, 769, 128) if cols % w == 0)
     total = (chips - 1) * chunks
     return pl.pallas_call(
         functools.partial(project_kernel, chips, share, chunks, width),
         out_shape=jax.ShapeDtypeStruct((2, tok, cols), jnp.bfloat16),
-        in_specs=[pl.BlockSpec(memory_space=pl.ANY)] * 2,
+        in_specs=[pl.BlockSpec(memory_space=pl.ANY)] * 3,
         out_specs=pl.BlockSpec(memory_space=pltpu.VMEM),
         scratch_shapes=[
             pltpu.VMEM((chips * 2 * tok, 2 * depth), jnp.bfloat16),
             pltpu.VMEM((2 * depth, cols), jnp.bfloat16),
             pltpu.VMEM((2, chips, 2 * tok, cols), jnp.bfloat16),
             pltpu.VMEM((tok, cols), jnp.bfloat16),
-            pltpu.SemaphoreType.DMA((2,)),
-            pltpu.SemaphoreType.DMA((2,)),
+            pltpu.SemaphoreType.DMA((3,)),
+            pltpu.SemaphoreType.DMA((4,)),
             pltpu.SemaphoreType.DMA((2,)),
             pltpu.SemaphoreType.DMA((2, chips)),
             pltpu.SemaphoreType.DMA((2, chips, share)),
@@ -255,7 +268,86 @@
         compiler_params=pltpu.CompilerParams(
             collective_id=0, has_side_effects=True, vmem_limit_bytes=48 * 1024 * 1024
         ),
-    )(tokens, weights)
+    )(tokens, weights, extra)
+
+
+def out_kernel(peers, width, n_ref, w_ref, out_ref, wbuf, held, landed, w_sem, send_sem, recv_sem):
+    f = lax.axis_index("fsdp")
+    h = lax.axis_index("head")
+    block = out_ref.shape[1]
+
+    def w_copy(o):
+        to = lax.rem(h + o, peers)
+        at = w_ref.at[:, pl.ds(pl.multiple_of(to * block, 128), block)]
+        return pltpu.make_async_copy(at, wbuf.at[o], w_sem.at[o])
+
+    def send(o):
+        return remote(held.at[o], landed.at[o], send_sem.at[o], recv_sem.at[o], f, lax.rem(h + o, peers))
+
+    for o in range(1, peers):
+        w_copy(o).start()
+    w_copy(0).start()
+    barrier = pltpu.get_barrier_semaphore()
+    for o in range(1, peers):
+        pl.semaphore_signal(barrier, inc=1, device_id=(f, lax.rem(h + o, peers)), device_id_type=MESH)
+    pl.semaphore_wait(barrier, peers - 1)
+
+    def columns(o, j):
+        to = pl.ds(pl.multiple_of(j * width, 128), width)
+        return to, jnp.dot(n_ref[...], wbuf[o, :, to], preferred_element_type=jnp.float32).astype(jnp.bfloat16)
+
+    @pl.loop(1, peers)
+    def _(o):
+        w_copy(o).wait()
+
+        @pl.loop(0, block // width)
+        def _(j):
+            to, value = columns(o, j)
+            held[o, :, to] = value
+
+        send(o).start()
+
+    w_copy(0).wait()
+
+    @pl.loop(0, block // width)
+    def _(j):
+        to, value = columns(0, j)
+        held[0, :, to] = value
+
+    @pl.loop(1, peers)
+    def _(o):
+        send(o).wait()
+
+    @pl.loop(0, block // width)
+    def _(j):
+        to = pl.ds(pl.multiple_of(j * width, 128), width)
+        total = held[0, :, to].astype(jnp.float32)
+        for o in range(1, peers):
+            total = total + landed[o, :, to].astype(jnp.float32)
+        out_ref[:, to] = total.astype(jnp.bfloat16)
+
+
+def out_project(normed, weight, n_head):
+    tok, rows = normed.shape
+    block = weight.shape[1] // n_head
+    width = 256 if block % 256 == 0 else 128
+    return pl.pallas_call(
+        functools.partial(out_kernel, n_head, width),
+        out_shape=jax.ShapeDtypeStruct((tok, block), jnp.bfloat16),
+        in_specs=[pl.BlockSpec(memory_space=pltpu.VMEM), pl.BlockSpec(memory_space=pl.ANY)],
+        out_specs=pl.BlockSpec(memory_space=pltpu.VMEM),
+        scratch_shapes=[
+            pltpu.VMEM((n_head, rows, block), jnp.bfloat16),
+            pltpu.VMEM((n_head, tok, block), jnp.bfloat16),
+            pltpu.VMEM((n_head, tok, block), jnp.bfloat16),
+            pltpu.SemaphoreType.DMA((n_head,)),
+            pltpu.SemaphoreType.DMA((n_head,)),
+            pltpu.SemaphoreType.DMA((n_head,)),
+        ],
+        compiler_params=pltpu.CompilerParams(
+            collective_id=1, has_side_effects=True, vmem_limit_bytes=40 * 1024 * 1024
+        ),
+    )(normed, weight)
 
 
 def causal(values, kernel, seq_len):
@@ -300,11 +392,10 @@
     used = zx_half + bc_half + dt_half
     cols = -(-used // 128) * 128
     blank = jnp.zeros((depth, cols - used), jnp.bfloat16)
-    weights = jnp.stack(
+    extra = jnp.stack(
         [
             jnp.concatenate(
                 [
-                    flat_zx[:, c * zx_half : (c + 1) * zx_half],
                     bc_part[:, c * bc_half : (c + 1) * bc_half],
                     dt_weight[:, c * dt_half : (c + 1) * dt_half],
                     blank,
@@ -314,7 +405,7 @@
             for c in (0, 1)
         ]
     )
-    got = project(tokens, weights, n_fsdp, n_head)
+    got = project(tokens, flat_zx, extra, n_fsdp, n_head)
     zx = jnp.concatenate([got[0, :, :zx_half], got[1, :, :zx_half]], axis=1).reshape(
         tok_rows, heads_here, 2, head_size
     )
@@ -352,10 +443,7 @@
         local_sq = jnp.sum(jnp.where(picks, totals, 0.0), axis=1)
     meansq = local_sq / (per_group * channels)
     normed = (gated / jnp.sqrt(meansq + 1e-05)[:, None] * norm_gain).astype(jnp.bfloat16)
-    partial_out = jnp.dot(normed, out_weight, preferred_element_type=jnp.float32)
-    return lax.psum_scatter(
-        partial_out.astype(jnp.bfloat16), "head", scatter_dimension=1, tiled=True
-    )
+    return out_project(normed, out_weight, n_head)
 
 
 def solution(mesh):

time: 310 us -> 282 us (0.910)
  waiting for transfers between devices: 33.5 us -> 0 us
  Pallas kernels: 210 us -> 241 us
  between operations: 13.6 us -> 0.23 us
  matrix products: 19.4 us -> 9.32 us
    reduce_scatter x1 -> x0, waiting for transfers between devices: 33.5 us -> none  [on_device(): lax.psum_scatter(partial_out.astype(jnp.bfloat16), 'head', scatter_dimens...]
    pallas_call x0 -> x1, Pallas kernels: none -> 30.6 us  [out_project(): pl.pallas_call(functools.partial(out_kernel, n_head, width), out_shape=ja...]
    dot_general x1 -> x0, matrix products: 11.6 us -> none  [on_device(): jnp.dot(normed, out_weight, preferred_element_type=jnp.float32)]
    concatenate x2 -> x1, local copies, waits for them, and re-layouts: 8.27 us -> 0.08 us  [on_device(): jnp.concatenate([bc_part[:, c * bc_half:(c + 1) * bc_half], dt_weight[:,...]
    another operation x1 -> x2, other arithmetic: 4.38 us -> 0.18 us  [on_device(): jnp.stack([jnp.concatenate([bc_part[:, c * bc_half:(c + 1) * bc_half], dt...]
    unnamed x13 -> x22, local copies, waits for them, and re-layouts: 6.96 us -> 9.83 us
  transfers between devices with their start and end apart: 1 -> 0, of which waited for: 1 -> 0; matrix products, arithmetic and copies ran while one was open for 0% -> 0% of each run, Pallas kernels for 0% -> 0%
where the time goes in v2:
time: 282 us
  Pallas kernels  241 us (85%)
  local copies, waits for them, and re-layouts  21.9 us (8%)
  matrix products  9.32 us (3%)
  other arithmetic  9.1 us (3%)
    pallas_call x1, Pallas kernels, project(): pl.pallas_call(functools.partial(project_kernel, chips, share, chunks, wi...  210 us
    pallas_call x1, Pallas kernels, out_project(): pl.pallas_call(functools.partial(out_kernel, n_head, width), out_shape=ja...  30.6 us
    unnamed x22, local copies, waits for them, and re-layouts  9.83 us
    dot_general x1, matrix products, on_device(): jnp.einsum('btsh,bshp->bthp', weights, xval, precision=lax.Precision.HIGH...  8.11 us

profile of v2, /device:TPU:10, one launch (start us, length us, event | category | flops | bytes accessed | tf_op | source)
XLA Modules:
  0.0 281.6 jit_solution(3232232347013388397)
XLA Ops:
  0.0 1.2 exp.43
  1.2 0.1 pad.23.clone
  1.3 0.9 constant_dynamic-slice_fusion
  2.2 1.5 fusion.42
  3.7 0.7 fusion.43
  4.5 0.7 iota_compare_fusion
  5.1 0.1 copy.29
  5.2 0.1 copy.30
  5.4 1.0 constant_dynamic-slice_fusion.1
  6.4 0.1 maximum_bitcast_fusion
  6.5 0.1 pad_maximum_fusion.1.e_ref
  6.6 0.0 copy-start
  6.6 8.5 %copy.45 = bf16[64,8,32,128]{3,1,2,0:T(8,128)(2,1)} copy(bf16[64,8,32,128]{3,2,1,0:T(8,128)(2,1)} %bitcast.76) | data formatting | bytes 8388608
  15.0 0.0 copy-done
  15.0 210.5 %shard_map.109 = bf16[2,256,2304]{2,1,0:T(8,128)(2,1)S(1)} custom-call(bf16[256,4096]{1,0:T(8,128)(2,1)S(1)} %copy-done, bf16[512,4096]{1,0:T(8,128)(2,1)} %bitcast.69, bf16[2,512,256]{2,1,0:T(8,128)(2,1)S(1)} %pad_maximum_fusion.1.e_ref), custom_call_target="tpu_custom_call" | custom-call | tf_op jit(solution)/shard_map/pallas_call | solution.py:248
  225.6 0.2 fusion.32
  225.8 0.2 fusion.33
  226.0 0.3 fusion.41
  226.3 0.5 copy.32
  226.8 0.0 copy-start.1
  226.8 0.1 copy.35
  226.9 0.1 copy.36
  226.9 1.0 convolution_bitcast_fusion
  228.0 0.7 compare_select_fusion
  228.7 0.5 copy.31
  229.3 0.0 copy-start.3
  229.3 1.6 fusion.29
  230.9 0.0 copy-done.1
  230.9 0.0 copy-done.3
  230.9 1.9 copy.38
  232.9 0.0 copy-start.6
  232.9 0.0 copy-start.7
  232.9 0.2 convert.4
  233.0 0.5 copy-done.6
  233.6 0.0 copy-done.7
  233.6 0.0 copy-start.2
  233.6 0.0 copy-start.4
  233.6 3.2 %fusion.30 = bf16[256,2048]{0,1:T(8,128)(2,1)S(1)} fusion(f32[1,256,2048]{1,2,0:T(8,128)S(1)} %convert.4, f32[2048]{0:T(1024)S(1)} %bitcast.82, f32[2048]{0:T(1024)S(1)} %bitcast.83, f32[2048]{0:T(1024)S(1)} %bitcast.81, f32[2048]{0:T(1024)S(1)} %bitcast.80), kind=kLoop, calls=%fused_computation.41 | loop fusion | flops 6291456 | bytes 3178496 | tf_op jit(solution)/shard_map/convert_element_type | solution.py:17
  236.8 0.0 copy-done.2
  236.8 0.0 copy-done.4
  236.8 0.0 copy-done.5
  236.8 0.0 copy-done.9
  236.8 8.1 %fusion.24 = (f32[256]{0:T(256)S(1)}, f32[1,256,32,64]{1,3,2,0:T(8,128)}) fusion(bf16[256,16,2,64]{0,3,2,1:T(8,128)(2,1)S(1)} %bitcast.73, bf16[256,16,2,64]{0,3,2,1:T(8,128)(2,1)S(1)} %bitcast.75, bf16[1,256,32,64]{1,3,2,0:T(8,128)(2,1)S(1)} %bitcast.78, f32[32]{0:T(128)S(1)} %copy-done.9, bf16[256,32,64]{0,2,1:T(8,128)(2,1)S(1)} %bitcast.79, ...), kind=kOutput, calls=%fused_computation.35 | convolution fusion | flops 1625292544 | bytes 6685824 | tf_op jit(solution)/shard_map/btsh,bshp->bthp/dot_general | solution.py:436
  244.9 2.9 %copy.39 = f32[256,2048]{1,0:T(8,128)} copy(f32[256,2048]{0,1:T(8,128)} %bitcast.77) | data formatting | bytes 4194304 | tf_op jit(solution)/shard_map/reshape | solution.py:438
  247.9 0.0 copy-done.8
  247.9 2.3 multiply_convert_fusion.n_ref
  250.2 30.6 %shard_map.110 = bf16[256,1024]{1,0:T(8,128)(2,1)S(1)} custom-call(bf16[256,2048]{1,0:T(8,128)(2,1)S(1)} %multiply_convert_fusion.n_ref, bf16[2048,4096]{1,0:T(8,128)(2,1)} %w_ref.1), custom_call_target="tpu_custom_call" | custom-call | tf_op jit(solution)/shard_map/pallas_call | solution.py:334
  280.8 0.8 copy.47
  (8 shorter events, 0.1 us)
Async XLA Ops:
  6.6 8.5 %copy-start = (bf16[256,4096]{1,0:T(8,128)(2,1)S(1)}, bf16[256,4096]{1,0:T(8,128)(2,1)}, u32[]{:S(2)}) copy-start(bf16[256,4096]{1,0:T(8,128)(2,1)} %tok_ref.1) | copy-start | bytes 6291460
  226.8 4.1 %copy-start.1 = (bf16[1,256,2048]{1,2,0:T(8,128)(2,1)}, bf16[1,256,2048]{1,2,0:T(8,128)(2,1)S(1)}, u32[]{:S(2)}) copy-start(bf16[1,256,2048]{1,2,0:T(8,128)(2,1)S(1)} %copy.32) | copy-start | bytes 3145732
  229.3 1.7 copy-start.3
  232.9 0.7 copy-start.6
  232.9 0.7 copy-start.7
  233.6 3.2 %copy-start.2 = (bf16[1,256,2048]{1,2,0:T(8,128)(2,1)S(1)}, bf16[1,256,2048]{1,2,0:T(8,128)(2,1)}, u32[]{:S(2)}) copy-start(bf16[1,256,2048]{1,2,0:T(8,128)(2,1)} %copy-done.1) | copy-start | bytes 3145732
  233.6 3.2 %copy-start.4 = (bf16[1,256,2048]{1,2,0:T(8,128)(2,1)S(1)}, bf16[1,256,2048]{1,2,0:T(8,128)(2,1)}, u32[]{:S(2)}) copy-start(bf16[1,256,2048]{1,2,0:T(8,128)(2,1)} %copy-done.3) | copy-start | bytes 3145732
  233.6 3.2 %copy-start.5 = (pred[256,256]{1,0:T(8,128)(4,1)S(1)}, pred[256,256]{1,0:T(8,128)(4,1)}, u32[]{:S(2)}) copy-start(pred[256,256]{1,0:T(8,128)(4,1)} %iota_compare_fusion) | copy-start | bytes 196612
  233.6 3.2 %copy-start.9 = (f32[32]{0:T(128)S(1)}, f32[32]{0:T(128)}, u32[]{:S(2)}) copy-start(f32[32]{0:T(128)} %param.19) | copy-start | bytes 388
  244.9 2.9 %copy-start.8 = (f32[2048]{0:T(1024)S(1)}, f32[2048]{0:T(1024)}, u32[]{:S(2)}) copy-start(f32[2048]{0:T(1024)} %param.20) | copy-start | bytes 24580

commit v3 on v2

--- a/solution.py
+++ b/solution.py
@@ -242,7 +242,7 @@
     tok = tokens.shape[0]
     depth = weights.shape[0]
     cols = weights.shape[1] // 2 + extra.shape[2]
-    chunks = 4
+    chunks = 8
     width = max(w for w in range(128, 769, 128) if cols % w == 0)
     total = (chips - 1) * chunks
     return pl.pallas_call(
@@ -433,7 +433,8 @@
     inner = jnp.einsum("btn,bsn->bts", cseq, bseq, preferred_element_type=jnp.float32)
     weights = inner[..., None] * decay * steps[:, None, :, :]
     xval = xconv.astype(jnp.float32).reshape(count, LEN, heads_here, head_size)
-    ys = jnp.einsum("btsh,bshp->bthp", weights, xval, precision=lax.Precision.HIGHEST)
+    xbf = xconv.reshape(count, LEN, heads_here, head_size)
+    ys = jnp.einsum("btsh,bshp->bthp", weights.astype(jnp.bfloat16), xbf, preferred_element_type=jnp.float32)
     ys = ys + d_skip[None, None, :, None] * xval
     gated = ys.reshape(tok_rows, channels) * jax.nn.silu(gate)
     local_sq = jnp.sum(gated * gated, axis=1)

time: 282 us -> 289 us (1.025)
  Pallas kernels: 241 us -> 252 us
  matrix products: 9.32 us -> 5.61 us
    pallas_call x1, Pallas kernels: 210 us -> 221 us  [project(): pl.pallas_call(functools.partial(project_kernel, chips, share, chunks, wi...]
    dot_general x1, matrix products: 8.11 us -> 4.4 us  [on_device(): jnp.einsum('btsh,bshp->bthp', weights.astype(jnp.bfloat16), xbf, preferre...]
where the time goes in v3:
time: 289 us
  Pallas kernels  252 us (87%)
  local copies, waits for them, and re-layouts  21.9 us (8%)
  other arithmetic  9.1 us (3%)
  matrix products  5.61 us (2%)
    pallas_call x1, Pallas kernels, project(): pl.pallas_call(functools.partial(project_kernel, chips, share, chunks, wi...  221 us
    pallas_call x1, Pallas kernels, out_project(): pl.pallas_call(functools.partial(out_kernel, n_head, width), out_shape=ja...  30.8 us
    unnamed x22, local copies, waits for them, and re-layouts  9.83 us

profile of v3, /device:TPU:10, one launch (start us, length us, event | category | flops | bytes accessed | tf_op | source)
XLA Modules:
  0.0 288.8 jit_solution(4149206542153421801)
XLA Ops:
  0.0 1.2 exp.43
  1.2 0.1 pad.23.clone
  1.3 0.9 constant_dynamic-slice_fusion
  2.2 1.5 fusion.35
  3.7 0.7 fusion.36
  4.5 0.7 iota_compare_fusion
  5.1 0.1 copy.29
  5.2 0.1 copy.30
  5.4 1.0 constant_dynamic-slice_fusion.1
  6.4 0.1 maximum_bitcast_fusion
  6.5 0.1 pad_maximum_fusion.1.e_ref
  6.6 0.0 copy-start
  6.6 8.5 %copy.45 = bf16[64,8,32,128]{3,1,2,0:T(8,128)(2,1)} copy(bf16[64,8,32,128]{3,2,1,0:T(8,128)(2,1)} %bitcast.76) | data formatting | bytes 8388608
  15.0 0.0 copy-done
  15.0 221.1 %shard_map.109 = bf16[2,256,2304]{2,1,0:T(8,128)(2,1)S(1)} custom-call(bf16[256,4096]{1,0:T(8,128)(2,1)S(1)} %copy-done, bf16[512,4096]{1,0:T(8,128)(2,1)} %bitcast.69, bf16[2,512,256]{2,1,0:T(8,128)(2,1)S(1)} %pad_maximum_fusion.1.e_ref), custom_call_target="tpu_custom_call" | custom-call | tf_op jit(solution)/shard_map/pallas_call | solution.py:248
  236.2 0.2 fusion.25
  236.4 0.2 fusion.26
  236.6 0.3 fusion.34
  236.9 0.5 copy.32
  237.4 0.0 copy-start.1
  237.4 0.1 copy.35
  237.5 0.1 copy.36
  237.6 1.0 convolution_bitcast_fusion
  238.6 0.7 compare_select_fusion
  239.4 0.5 copy.31
  239.9 0.0 copy-start.3
  239.9 1.6 fusion.22
  241.6 0.0 copy-done.1
  241.6 0.0 copy-done.3
  241.6 1.9 copy.38
  243.5 0.0 copy-start.6
  243.5 0.0 copy-start.7
  243.5 0.2 convert.4
  243.7 0.5 copy-done.6
  244.2 0.0 copy-done.7
  244.2 0.0 copy-start.2
  244.2 0.0 copy-start.4
  244.2 3.2 %fusion.23 = bf16[256,2048]{0,1:T(8,128)(2,1)S(1)} fusion(f32[1,256,2048]{1,2,0:T(8,128)S(1)} %convert.4, f32[2048]{0:T(1024)S(1)} %bitcast.82, f32[2048]{0:T(1024)S(1)} %bitcast.83, f32[2048]{0:T(1024)S(1)} %bitcast.81, f32[2048]{0:T(1024)S(1)} %bitcast.80), kind=kLoop, calls=%fused_computation.37 | loop fusion | flops 6291456 | bytes 3178496 | tf_op jit(solution)/shard_map/convert_element_type | solution.py:17
  247.4 0.0 copy-done.2
  247.4 0.0 copy-done.4
  247.4 0.0 copy-done.5
  247.4 0.0 copy-done.9
  247.5 4.4 %fusion.19 = (f32[256]{0:T(256)S(1)}, f32[1,256,32,64]{1,3,2,0:T(8,128)}) fusion(bf16[256,16,2,64]{0,3,2,1:T(8,128)(2,1)S(1)} %bitcast.73, bf16[256,16,2,64]{0,3,2,1:T(8,128)(2,1)S(1)} %bitcast.75, bf16[1,256,32,64]{1,3,2,0:T(8,128)(2,1)S(1)} %bitcast.78, f32[32]{0:T(128)S(1)} %copy-done.9, bf16[256,32,64]{0,2,1:T(8,128)(2,1)S(1)} %bitcast.79, ...), kind=kOutput, calls=%fused_computation.31 | convolution fusion | flops 285212416 | bytes 6685824 | tf_op jit(solution)/shard_map/btsh,bshp->bthp/dot_general | solution.py:437
  251.9 2.9 %copy.39 = f32[256,2048]{1,0:T(8,128)} copy(f32[256,2048]{0,1:T(8,128)} %bitcast.77) | data formatting | bytes 4194304 | tf_op jit(solution)/shard_map/reshape | solution.py:439
  254.8 0.0 copy-done.8
  254.8 2.3 multiply_convert_fusion.2.n_ref
  257.1 30.8 %shard_map.110 = bf16[256,1024]{1,0:T(8,128)(2,1)S(1)} custom-call(bf16[256,2048]{1,0:T(8,128)(2,1)S(1)} %multiply_convert_fusion.2.n_ref, bf16[2048,4096]{1,0:T(8,128)(2,1)} %w_ref.1), custom_call_target="tpu_custom_call" | custom-call | tf_op jit(solution)/shard_map/pallas_call | solution.py:334
  288.0 0.8 copy.47
  (8 shorter events, 0.1 us)
Async XLA Ops:
  6.6 8.5 %copy-start = (bf16[256,4096]{1,0:T(8,128)(2,1)S(1)}, bf16[256,4096]{1,0:T(8,128)(2,1)}, u32[]{:S(2)}) copy-start(bf16[256,4096]{1,0:T(8,128)(2,1)} %tok_ref.1) | copy-start | bytes 6291460
  237.4 4.1 %copy-start.1 = (bf16[1,256,2048]{1,2,0:T(8,128)(2,1)}, bf16[1,256,2048]{1,2,0:T(8,128)(2,1)S(1)}, u32[]{:S(2)}) copy-start(bf16[1,256,2048]{1,2,0:T(8,128)(2,1)S(1)} %copy.32) | copy-start | bytes 3145732
  239.9 1.7 copy-start.3
  243.5 0.7 copy-start.6
  243.5 0.7 copy-start.7
  244.2 3.2 %copy-start.2 = (bf16[1,256,2048]{1,2,0:T(8,128)(2,1)S(1)}, bf16[1,256,2048]{1,2,0:T(8,128)(2,1)}, u32[]{:S(2)}) copy-start(bf16[1,256,2048]{1,2,0:T(8,128)(2,1)} %copy-done.1) | copy-start | bytes 3145732
  244.2 3.2 %copy-start.4 = (bf16[1,256,2048]{1,2,0:T(8,128)(2,1)S(1)}, bf16[1,256,2048]{1,2,0:T(8,128)(2,1)}, u32[]{:S(2)}) copy-start(bf16[1,256,2048]{1,2,0:T(8,128)(2,1)} %copy-done.3) | copy-start | bytes 3145732
  244.2 3.2 %copy-start.5 = (pred[256,256]{1,0:T(8,128)(4,1)S(1)}, pred[256,256]{1,0:T(8,128)(4,1)}, u32[]{:S(2)}) copy-start(pred[256,256]{1,0:T(8,128)(4,1)} %iota_compare_fusion) | copy-start | bytes 196612
  244.2 3.2 %copy-start.9 = (f32[32]{0:T(128)S(1)}, f32[32]{0:T(128)}, u32[]{:S(2)}) copy-start(f32[32]{0:T(128)} %param.19) | copy-start | bytes 388
  251.9 2.9 %copy-start.8 = (f32[2048]{0:T(1024)S(1)}, f32[2048]{0:T(1024)}, u32[]{:S(2)}) copy-start(f32[2048]{0:T(1024)} %param.20) | copy-start | bytes 24580

commit v4 on v3

--- a/solution.py
+++ b/solution.py
@@ -242,7 +242,7 @@
     tok = tokens.shape[0]
     depth = weights.shape[0]
     cols = weights.shape[1] // 2 + extra.shape[2]
-    chunks = 8
+    chunks = 4
     width = max(w for w in range(128, 769, 128) if cols % w == 0)
     total = (chips - 1) * chunks
     return pl.pallas_call(

time: 289 us -> 278 us (0.962)
  Pallas kernels: 252 us -> 241 us
    pallas_call x1, Pallas kernels: 221 us -> 210 us  [project(): pl.pallas_call(functools.partial(project_kernel, chips, share, chunks, wi...]
where the time goes in v4:
time: 278 us
  Pallas kernels  241 us (87%)
  local copies, waits for them, and re-layouts  21.9 us (8%)
  other arithmetic  9.1 us (3%)
  matrix products  5.61 us (2%)
    pallas_call x1, Pallas kernels, project(): pl.pallas_call(functools.partial(project_kernel, chips, share, chunks, wi...  210 us
    pallas_call x1, Pallas kernels, out_project(): pl.pallas_call(functools.partial(out_kernel, n_head, width), out_shape=ja...  30.6 us
    unnamed x22, local copies, waits for them, and re-layouts  9.83 us

profile of v4, /device:TPU:10, one launch (start us, length us, event | category | flops | bytes accessed | tf_op | source)
XLA Modules:
  0.0 277.9 jit_solution(6532555150618949965)
XLA Ops:
  0.0 1.2 exp.43
  1.2 0.1 pad.23.clone
  1.3 0.9 constant_dynamic-slice_fusion
  2.2 1.5 fusion.35
  3.7 0.7 fusion.36
  4.5 0.7 iota_compare_fusion
  5.1 0.1 copy.29
  5.2 0.1 copy.30
  5.4 1.0 constant_dynamic-slice_fusion.1
  6.4 0.1 maximum_bitcast_fusion
  6.5 0.1 pad_maximum_fusion.1.e_ref
  6.6 0.0 copy-start
  6.6 8.5 %copy.45 = bf16[64,8,32,128]{3,1,2,0:T(8,128)(2,1)} copy(bf16[64,8,32,128]{3,2,1,0:T(8,128)(2,1)} %bitcast.76) | data formatting | bytes 8388608
  15.0 0.0 copy-done
  15.0 210.5 %shard_map.109 = bf16[2,256,2304]{2,1,0:T(8,128)(2,1)S(1)} custom-call(bf16[256,4096]{1,0:T(8,128)(2,1)S(1)} %copy-done, bf16[512,4096]{1,0:T(8,128)(2,1)} %bitcast.69, bf16[2,512,256]{2,1,0:T(8,128)(2,1)S(1)} %pad_maximum_fusion.1.e_ref), custom_call_target="tpu_custom_call" | custom-call | tf_op jit(solution)/shard_map/pallas_call | solution.py:248
  225.6 0.2 fusion.25
  225.8 0.2 fusion.26
  226.0 0.3 fusion.34
  226.3 0.5 copy.32
  226.8 0.0 copy-start.1
  226.8 0.1 copy.35
  226.9 0.1 copy.36
  226.9 1.0 convolution_bitcast_fusion
  228.0 0.7 compare_select_fusion
  228.7 0.5 copy.31
  229.3 0.0 copy-start.3
  229.3 1.6 fusion.22
  230.9 0.0 copy-done.1
  230.9 0.0 copy-done.3
  230.9 1.9 copy.38
  232.9 0.0 copy-start.6
  232.9 0.0 copy-start.7
  232.9 0.2 convert.4
  233.0 0.5 copy-done.6
  233.6 0.0 copy-done.7
  233.6 0.0 copy-start.2
  233.6 0.0 copy-start.4
  233.6 3.2 %fusion.23 = bf16[256,2048]{0,1:T(8,128)(2,1)S(1)} fusion(f32[1,256,2048]{1,2,0:T(8,128)S(1)} %convert.4, f32[2048]{0:T(1024)S(1)} %bitcast.82, f32[2048]{0:T(1024)S(1)} %bitcast.83, f32[2048]{0:T(1024)S(1)} %bitcast.81, f32[2048]{0:T(1024)S(1)} %bitcast.80), kind=kLoop, calls=%fused_computation.37 | loop fusion | flops 6291456 | bytes 3178496 | tf_op jit(solution)/shard_map/convert_element_type | solution.py:17
  236.8 0.0 copy-done.2
  236.8 0.0 copy-done.4
  236.8 0.0 copy-done.5
  236.8 0.0 copy-done.9
  236.8 4.4 %fusion.19 = (f32[256]{0:T(256)S(1)}, f32[1,256,32,64]{1,3,2,0:T(8,128)}) fusion(bf16[256,16,2,64]{0,3,2,1:T(8,128)(2,1)S(1)} %bitcast.73, bf16[256,16,2,64]{0,3,2,1:T(8,128)(2,1)S(1)} %bitcast.75, bf16[1,256,32,64]{1,3,2,0:T(8,128)(2,1)S(1)} %bitcast.78, f32[32]{0:T(128)S(1)} %copy-done.9, bf16[256,32,64]{0,2,1:T(8,128)(2,1)S(1)} %bitcast.79, ...), kind=kOutput, calls=%fused_computation.31 | convolution fusion | flops 285212416 | bytes 6685824 | tf_op jit(solution)/shard_map/btsh,bshp->bthp/dot_general | solution.py:437
  241.2 2.9 %copy.39 = f32[256,2048]{1,0:T(8,128)} copy(f32[256,2048]{0,1:T(8,128)} %bitcast.77) | data formatting | bytes 4194304 | tf_op jit(solution)/shard_map/reshape | solution.py:439
  244.2 0.0 copy-done.8
  244.2 2.3 multiply_convert_fusion.2.n_ref
  246.5 30.6 %shard_map.110 = bf16[256,1024]{1,0:T(8,128)(2,1)S(1)} custom-call(bf16[256,2048]{1,0:T(8,128)(2,1)S(1)} %multiply_convert_fusion.2.n_ref, bf16[2048,4096]{1,0:T(8,128)(2,1)} %w_ref.1), custom_call_target="tpu_custom_call" | custom-call | tf_op jit(solution)/shard_map/pallas_call | solution.py:334
  277.1 0.8 copy.47
  (8 shorter events, 0.1 us)
Async XLA Ops:
  6.6 8.5 %copy-start = (bf16[256,4096]{1,0:T(8,128)(2,1)S(1)}, bf16[256,4096]{1,0:T(8,128)(2,1)}, u32[]{:S(2)}) copy-start(bf16[256,4096]{1,0:T(8,128)(2,1)} %tok_ref.1) | copy-start | bytes 6291460
  226.8 4.1 %copy-start.1 = (bf16[1,256,2048]{1,2,0:T(8,128)(2,1)}, bf16[1,256,2048]{1,2,0:T(8,128)(2,1)S(1)}, u32[]{:S(2)}) copy-start(bf16[1,256,2048]{1,2,0:T(8,128)(2,1)S(1)} %copy.32) | copy-start | bytes 3145732
  229.3 1.7 copy-start.3
  232.9 0.7 copy-start.6
  232.9 0.7 copy-start.7
  233.6 3.2 %copy-start.2 = (bf16[1,256,2048]{1,2,0:T(8,128)(2,1)S(1)}, bf16[1,256,2048]{1,2,0:T(8,128)(2,1)}, u32[]{:S(2)}) copy-start(bf16[1,256,2048]{1,2,0:T(8,128)(2,1)} %copy-done.1) | copy-start | bytes 3145732
  233.6 3.2 %copy-start.4 = (bf16[1,256,2048]{1,2,0:T(8,128)(2,1)S(1)}, bf16[1,256,2048]{1,2,0:T(8,128)(2,1)}, u32[]{:S(2)}) copy-start(bf16[1,256,2048]{1,2,0:T(8,128)(2,1)} %copy-done.3) | copy-start | bytes 3145732
  233.6 3.2 %copy-start.5 = (pred[256,256]{1,0:T(8,128)(4,1)S(1)}, pred[256,256]{1,0:T(8,128)(4,1)}, u32[]{:S(2)}) copy-start(pred[256,256]{1,0:T(8,128)(4,1)} %iota_compare_fusion) | copy-start | bytes 196612
  233.6 3.2 %copy-start.9 = (f32[32]{0:T(128)S(1)}, f32[32]{0:T(128)}, u32[]{:S(2)}) copy-start(f32[32]{0:T(128)} %param.19) | copy-start | bytes 388
  241.2 2.9 %copy-start.8 = (f32[2048]{0:T(1024)S(1)}, f32[2048]{0:T(1024)}, u32[]{:S(2)}) copy-start(f32[2048]{0:T(1024)} %param.20) | copy-start | bytes 24580
